TPU v7x, 32 devices: a whole 2x2x4 slice. The times are simulated.
32 devices in a mesh: dp: 8 (over z, x), chan: 4 (over y, core).
Axes of the slice: x: 2, y: 2, z: 4, core: 2. Of those that a mesh axis runs over, the one named last changes fastest.
Arguments:
- images: bfloat16 [256, 7, 7, 2048], P('dp'), may hold values from -6 to 6
- crop_image: int32 [256], P('dp'), may hold values from 0 to 15
- slot_rows: int32 [4096], replicated, may hold values from 0 to 2048, as said below
- squeeze_weight: float32 [4096, 512], P('dp', 'chan'), may hold values from -0.125 to 0.125
- squeeze_moment: float32 [4096, 512], P('dp', 'chan'), may hold values from -320 to 320
- squeeze_second: float32 [4096, 512], P('dp', 'chan'), may hold values from 2829.9302 to 11319.721
- spatial_weight: float32 [4608, 512], P('dp', 'chan'), may hold values from -0.09375 to 0.09375
- spatial_moment: float32 [4608, 512], P('dp', 'chan'), may hold values from -256 to 256
- spatial_second: float32 [4608, 512], P('dp', 'chan'), may hold values from 1599.999 to 6399.996
- expand_weight: float32 [4096, 512], P('dp', 'chan'), may hold values from -0.25 to 0.25
- expand_moment: float32 [4096, 512], P('dp', 'chan'), may hold values from -128 to 128
- expand_second: float32 [4096, 512], P('dp', 'chan'), may hold values from 399.99976 to 1599.999
- hidden_weight: float32 [4096, 2048], P('dp', 'chan'), may hold values from -0.125 to 0.125
- hidden_moment: float32 [4096, 2048], P('dp', 'chan'), may hold values from -160 to 160
- hidden_second: float32 [4096, 2048], P('dp', 'chan'), may hold values from 799.9995 to 3199.998
- project_weight: float32 [4096, 128], P('dp'), may hold values from -0.125 to 0.125
- project_moment: float32 [4096, 128], P('dp'), may hold values from -640 to 640
- project_second: float32 [4096, 128], P('dp'), may hold values from 13866.658 to 55466.633
- prototypes: float32 [128, 3000], replicated, may hold values from -0.2 to 0.2
- proto_moment: float32 [128, 3000], replicated, may hold values from -112 to 112
- proto_second: float32 [128, 3000], replicated, may hold values from 355.55533 to 1422.2213
- norm_params: float32 [2, 4, 1280], P(None, 'chan'), may hold values from 0.25 to 1.75
- norm_moment: float32 [2, 4, 1280], P(None, 'chan'), may hold values from -139.9708 to 139.9708
- norm_second: float32 [2, 4, 1280], P(None, 'chan'), may hold values from 272.10867 to 8707.478
- queue_rows: bfloat16 [3840, 128], P('dp'), may hold values from -1.25 to 1.25
- queue_valid: int32 [3840], P('dp'), may hold values 0 or 1
- queue_fill: int32 [1], replicated, may hold values from 960 to 3839
- iteration: int32 [1], replicated, may hold values from 1 to 4
Outputs:
- block_out: bfloat16 [256, 7, 7, 2048], P('dp', None, None, 'chan')
- loss: float32 [1], replicated
- images_grad: float32 [256, 7, 7, 2048], P('dp', None, None, 'chan')
- squeeze_weight_new: float32 [4096, 512], P('dp', 'chan')
- squeeze_moment_new: float32 [4096, 512], P('dp', 'chan')
- squeeze_second_new: float32 [4096, 512], P('dp', 'chan')
- spatial_weight_new: float32 [4608, 512], P('dp', 'chan')
- spatial_moment_new: float32 [4608, 512], P('dp', 'chan')
- spatial_second_new: float32 [4608, 512], P('dp', 'chan')
- expand_weight_new: float32 [4096, 512], P('dp', 'chan')
- expand_moment_new: float32 [4096, 512], P('dp', 'chan')
- expand_second_new: float32 [4096, 512], P('dp', 'chan')
- hidden_weight_new: float32 [4096, 2048], P('dp', 'chan')
- hidden_moment_new: float32 [4096, 2048], P('dp', 'chan')
- hidden_second_new: float32 [4096, 2048], P('dp', 'chan')
- project_weight_new: float32 [4096, 128], P('dp')
- project_moment_new: float32 [4096, 128], P('dp')
- project_second_new: float32 [4096, 128], P('dp')
- prototypes_new: float32 [128, 3000], replicated
- proto_moment_new: float32 [128, 3000], replicated
- proto_second_new: float32 [128, 3000], replicated
- norm_params_new: float32 [2, 4, 1280], P(None, 'chan')
- norm_moment_new: float32 [2, 4, 1280], P(None, 'chan')
- norm_second_new: float32 [2, 4, 1280], P(None, 'chan')
Inputs may be any that keep to these rules, and one draw needn't show every extreme that they name: `slot_rows`: every channel 0 to 2047 stands in exactly one slot; the value 2048 marks an empty slot. Slots k * 512 onward belong to owner k of dp; loads are uneven, and one owner's slots are all used in every draw. `crop_image`: crops with the same label in one device's block of 32 crops are views of one image.
All inputs are finite; a program needn't handle non-finite values. No bound on the sum of `queue_valid` on one device may be relied on, other than what follows from the above.
Results may differ from a plain program's by a relative error of at most 0.028.
Values may be sent and summed in bfloat16 or wider, within the bound.
No kernel may reach another device: no remote copies, remote signals or barrier semaphores. Data moves between devices by JAX's collectives and lax.ppermute only.
A program may use at most 256 MiB of HBM per device.

v0:
```python
import jax
import jax.numpy as jnp
from jax import lax
from jax.sharding import PartitionSpec as P

C_IN = 2048
C_MID = 512
HID = 2048
SINK_ITERS = 3


PRECISE = lax.Precision.HIGHEST
EPS_SINK = 0.05
SOFTMAX_WARMTH = 0.1
LOSS_MULTIPLIER = 256.0
NORM_EPS = 1e-05
BETA_ONE = 0.5
BETA_TWO = 0.5
ADAM_EPS = 1e-08
DECAY_RATE = 1e-06


def contract(left, right, left_dim, right_dim):
    return lax.dot_general(
        left, right, (((left_dim,), (right_dim,)), ((), ())), preferred_element_type=jnp.float32
    )


def silu_slope(value):
    sigma = jax.nn.sigmoid(value)
    return sigma * (1.0 + value * (1.0 - sigma))


def image_sums(first_term, second_term):
    return lax.psum((first_term, second_term), "dp")


def norm_forward(pre_act, gain_row, bias_row, row_total):
    sum_one, sum_two = image_sums(jnp.sum(pre_act, axis=0), jnp.sum(pre_act * pre_act, axis=0))
    average = sum_one / row_total
    variance = sum_two / row_total - average * average
    inv_std = lax.rsqrt(variance + NORM_EPS)
    centred = (pre_act - average) * inv_std
    return (centred * gain_row + bias_row, centred, inv_std)


def norm_backward(grad_out, centred, inv_std, gain_row, row_total):
    bias_grad, gain_grad = image_sums(
        jnp.sum(grad_out, axis=0), jnp.sum(grad_out * centred, axis=0)
    )
    grad_in = gain_row * inv_std * (grad_out - (bias_grad + centred * gain_grad) / row_total)
    return (grad_in, gain_grad, bias_grad)


def patch_rows(inner, crops_dev, map_side, width):
    feature_maps = inner.reshape(crops_dev, map_side, map_side, width)
    padded = jnp.pad(feature_maps, ((0, 0), (1, 1), (1, 1), (0, 0)))
    tap_list = [
        padded[:, row_at : row_at + map_side, col_at : col_at + map_side, :]
        for row_at in range(3)
        for col_at in range(3)
    ]
    return jnp.concatenate(tap_list, axis=3).reshape(crops_dev * map_side * map_side, 9 * width)


def patch_back(column_grad, crops_dev, map_side, width):
    tap_grads = column_grad.reshape(crops_dev, map_side, map_side, 9, width)
    padded = jnp.zeros((crops_dev, map_side + 2, map_side + 2, width), jnp.float32)
    for row_at in range(3):
        for col_at in range(3):
            padded = padded.at[:, row_at : row_at + map_side, col_at : col_at + map_side, :].add(
                tap_grads[:, :, :, row_at * 3 + col_at, :]
            )
    return padded[:, 1:-1, 1:-1, :].reshape(crops_dev * map_side * map_side, width)


def adamw_step(weight, moment_one, moment_two, gradient, learn_rate, weight_decay, step_count):
    moment_new = BETA_ONE * moment_one + (1.0 - BETA_ONE) * gradient
    second_new = BETA_TWO * moment_two + (1.0 - BETA_TWO) * gradient * gradient
    fix_one = 1.0 - jnp.power(BETA_ONE, step_count)
    fix_two = 1.0 - jnp.power(BETA_TWO, step_count)
    update = moment_new / fix_one / (jnp.sqrt(second_new / fix_two) + ADAM_EPS)
    return (weight - learn_rate * (update + weight_decay * weight), moment_new, second_new)


def local(
    images,
    crop_image,
    slot_rows,
    squeeze_weight,
    squeeze_moment,
    squeeze_second,
    spatial_weight,
    spatial_moment,
    spatial_second,
    expand_weight,
    expand_moment,
    expand_second,
    hidden_weight,
    hidden_moment,
    hidden_second,
    project_weight,
    project_moment,
    project_second,
    prototypes,
    proto_moment,
    proto_second,
    norm_params,
    norm_moment,
    norm_second,
    queue_rows,
    queue_valid,
    queue_fill,
    iteration,
):
    dp_count = lax.axis_size("dp")
    dp_at = lax.axis_index("dp")
    chan_count = lax.axis_size("chan")
    chan_at = lax.axis_index("chan")
    crops_dev = images.shape[0]
    map_side = images.shape[1]
    map_area = map_side * map_side
    in_width = images.shape[3]
    pixel_rows = crops_dev * map_area
    pixel_total = pixel_rows * dp_count
    crop_total = crops_dev * dp_count
    mid_local = squeeze_weight.shape[1]
    hid_local = hidden_weight.shape[1]
    out_local = in_width // chan_count
    slot_total = slot_rows.shape[0]
    mid_width = mid_local * chan_count
    gathered = (
        lax.all_gather(squeeze_weight.astype(jnp.bfloat16), "dp", axis=0, tiled=True),
        lax.all_gather(expand_weight.astype(jnp.bfloat16), "dp", axis=0, tiled=True),
        lax.all_gather(hidden_weight.astype(jnp.bfloat16), "dp", axis=0, tiled=True),
        lax.all_gather(project_weight.astype(jnp.bfloat16), "dp", axis=0, tiled=True),
        lax.all_gather(spatial_weight.astype(jnp.bfloat16), "dp", axis=0, tiled=True),
    )
    row_place = (
        jnp.zeros((in_width + 1,), jnp.int32)
        .at[slot_rows]
        .set(jnp.arange(slot_total, dtype=jnp.int32))[:in_width]
    )
    squeeze_rows = gathered[0][row_place]
    expand_rows = gathered[1][row_place]
    hidden_rows = gathered[2][row_place]
    project_rows = gathered[3][row_place]
    spatial_full = gathered[4]
    norm_rows = norm_params[:, 0, :]
    first_norm = norm_rows[:, :mid_local]
    second_norm = norm_rows[:, mid_local : 2 * mid_local]
    third_norm = norm_rows[:, 2 * mid_local : 2 * mid_local + out_local]
    head_norm = norm_rows[:, 2 * mid_local + out_local :]
    pixels = images.reshape(pixel_rows, in_width)
    pre_one = jnp.dot(pixels, squeeze_rows, preferred_element_type=jnp.float32)
    normed_one, centred_one, inv_one = norm_forward(
        pre_one, first_norm[0], first_norm[1], pixel_total
    )
    inner_one = jax.nn.silu(normed_one).astype(jnp.bfloat16)
    inner_all = lax.all_gather(inner_one, "chan", axis=1, tiled=True)
    columns = patch_rows(inner_all, crops_dev, map_side, mid_width)
    pre_two = jnp.dot(columns, spatial_full, preferred_element_type=jnp.float32)
    normed_two, centred_two, inv_two = norm_forward(
        pre_two, second_norm[0], second_norm[1], pixel_total
    )
    inner_two = jax.nn.silu(normed_two).astype(jnp.bfloat16)
    expand_terms = contract(inner_two, expand_rows, 1, 1)
    pre_three = lax.psum_scatter(expand_terms, "chan", scatter_dimension=1, tiled=True)
    normed_three, centred_three, inv_three = norm_forward(
        pre_three, third_norm[0], third_norm[1], pixel_total
    )
    residual_in = lax.dynamic_slice_in_dim(pixels, chan_at * out_local, out_local, 1).astype(
        jnp.float32
    )
    summed = normed_three + residual_in
    block_rows = jax.nn.silu(summed)
    block_out = block_rows.astype(jnp.bfloat16).reshape(crops_dev, map_side, map_side, out_local)
    pooled = jnp.mean(block_rows.reshape(crops_dev, map_area, out_local), axis=1).astype(
        jnp.bfloat16
    )
    pooled_all = lax.all_gather(pooled, "chan", axis=1, tiled=True)
    hidden_pre = jnp.dot(pooled_all, hidden_rows, preferred_element_type=jnp.float32)
    normed_head, centred_head, inv_head = norm_forward(
        hidden_pre, head_norm[0], head_norm[1], crop_total
    )
    hidden_act = jax.nn.silu(normed_head).astype(jnp.bfloat16)
    hidden_all = lax.all_gather(hidden_act, "chan", axis=1, tiled=True)
    project_out = jnp.dot(hidden_all, project_rows, preferred_element_type=jnp.float32)
    inv_len = lax.rsqrt(jnp.sum(project_out * project_out, axis=1, keepdims=True) + 1e-06)
    normed = project_out * inv_len
    normed_low = normed.astype(jnp.bfloat16)
    proto_low = prototypes.astype(jnp.bfloat16)
    prototype_scores = jnp.dot(normed_low, proto_low, preferred_element_type=jnp.float32)
    queue_similarity = jnp.dot(queue_rows, proto_low, preferred_element_type=jnp.float32)
    queue_len = queue_rows.shape[0]
    slot_index = dp_at * queue_len + jnp.arange(queue_len, dtype=jnp.int32)
    queue_active = ((queue_valid > 0) & (slot_index < queue_fill[0])).astype(jnp.float32)
    batch_codes = jnp.exp(prototype_scores / EPS_SINK)
    queue_codes = jnp.exp(queue_similarity / EPS_SINK) * queue_active[:, None]
    for turn_index in range(SINK_ITERS):
        proto_totals = lax.psum(jnp.sum(batch_codes, axis=0) + jnp.sum(queue_codes, axis=0), "dp")
        batch_codes = batch_codes / proto_totals
        queue_codes = queue_codes / proto_totals
        batch_codes = batch_codes / jnp.sum(batch_codes, axis=1, keepdims=True)
        queue_sums = jnp.sum(queue_codes, axis=1, keepdims=True)
        queue_codes = queue_codes / jnp.where(queue_active[:, None] > 0, queue_sums, 1.0)
    crop_index = jnp.arange(crops_dev, dtype=jnp.int32)
    same_image = (crop_image[:, None] == crop_image[None, :]) & (
        crop_index[:, None] != crop_index[None, :]
    )
    pair_weights = same_image.astype(jnp.float32)
    others = jnp.sum(pair_weights, axis=1, keepdims=True)
    target_rows = jnp.dot(pair_weights, batch_codes, precision=PRECISE) / jnp.maximum(others, 1.0)
    raw_scores = prototype_scores / SOFTMAX_WARMTH
    log_norm = jax.nn.logsumexp(raw_scores, axis=1, keepdims=True)
    log_likelihoods = raw_scores - log_norm
    per_crop = -jnp.sum(target_rows * log_likelihoods, axis=1)
    target_weight_total = jnp.sum(target_rows, axis=1, keepdims=True)
    score_gradient = (
        LOSS_MULTIPLIER
        / SOFTMAX_WARMTH
        * (jnp.exp(log_likelihoods) * target_weight_total - target_rows)
    ).astype(jnp.bfloat16)
    proto_local = contract(normed_low, score_gradient, 0, 0)
    proto_grad, loss_total = lax.psum((proto_local, jnp.sum(per_crop).reshape(1)), "dp")
    loss = loss_total / crop_total
    normed_grad = contract(score_gradient, proto_low, 1, 1)
    project_low_grad = (
        inv_len * (normed_grad - normed * jnp.sum(normed * normed_grad, axis=1, keepdims=True))
    ).astype(jnp.bfloat16)
    project_grad = contract(hidden_all, project_low_grad, 0, 0)
    project_part = lax.dynamic_slice_in_dim(project_rows, chan_at * hid_local, hid_local, 0)
    hidden_grad_act = contract(project_low_grad, project_part, 1, 1) * silu_slope(normed_head)
    head_pre_grad, head_gain_grad, head_bias_grad = norm_backward(
        hidden_grad_act, centred_head, inv_head, head_norm[0], crop_total
    )
    head_pre_low = head_pre_grad.astype(jnp.bfloat16)
    hidden_grad = contract(pooled_all, head_pre_low, 0, 0)
    pooled_terms = contract(head_pre_low, hidden_rows, 1, 1)
    pooled_grad = lax.psum_scatter(pooled_terms, "chan", scatter_dimension=1, tiled=True)
    spread_grad = jnp.broadcast_to(
        pooled_grad[:, None, :] / map_area, (crops_dev, map_area, out_local)
    ).reshape(pixel_rows, out_local)
    sum_grad = spread_grad * silu_slope(summed)
    third_grad, third_gain_grad, third_bias_grad = norm_backward(
        sum_grad, centred_three, inv_three, third_norm[0], pixel_total
    )
    third_low = third_grad.astype(jnp.bfloat16)
    third_all = lax.all_gather(third_low, "chan", axis=1, tiled=True)
    expand_grad = contract(third_all, inner_two, 0, 0)
    inner_two_grad = jnp.dot(
        third_all, expand_rows, preferred_element_type=jnp.float32
    ) * silu_slope(normed_two)
    second_grad, second_gain_grad, second_bias_grad = norm_backward(
        inner_two_grad, centred_two, inv_two, second_norm[0], pixel_total
    )
    second_low = second_grad.astype(jnp.bfloat16)
    spatial_grad = contract(columns, second_low, 0, 0)
    column_grad = contract(second_low, spatial_full, 1, 1)
    inner_terms = patch_back(column_grad, crops_dev, map_side, mid_width)
    inner_one_grad = lax.psum_scatter(
        inner_terms, "chan", scatter_dimension=1, tiled=True
    ) * silu_slope(normed_one)
    first_grad, first_gain_grad, first_bias_grad = norm_backward(
        inner_one_grad, centred_one, inv_one, first_norm[0], pixel_total
    )
    first_low = first_grad.astype(jnp.bfloat16)
    squeeze_grad = contract(pixels, first_low, 0, 0)
    input_terms = contract(first_low, squeeze_rows, 1, 1)
    input_sum = lax.psum_scatter(input_terms, "chan", scatter_dimension=1, tiled=True)
    images_grad = (input_sum + sum_grad).reshape(crops_dev, map_side, map_side, out_local)

    def pad_rows(grad_rows):
        return jnp.concatenate([grad_rows, jnp.zeros((1, grad_rows.shape[1]), jnp.float32)], axis=0)

    slot_squeeze, slot_expand, slot_hidden, slot_project, slot_spatial = (
        lax.psum_scatter(pad_rows(squeeze_grad)[slot_rows], "dp", scatter_dimension=0, tiled=True),
        lax.psum_scatter(pad_rows(expand_grad)[slot_rows], "dp", scatter_dimension=0, tiled=True),
        lax.psum_scatter(pad_rows(hidden_grad)[slot_rows], "dp", scatter_dimension=0, tiled=True),
        lax.psum_scatter(pad_rows(project_grad)[slot_rows], "dp", scatter_dimension=0, tiled=True),
        lax.psum_scatter(spatial_grad, "dp", scatter_dimension=0, tiled=True),
    )
    gain_grads = jnp.concatenate(
        [first_gain_grad, second_gain_grad, third_gain_grad, head_gain_grad]
    )
    bias_grads = jnp.concatenate(
        [first_bias_grad, second_bias_grad, third_bias_grad, head_bias_grad]
    )
    norm_gradient = jnp.stack([gain_grads, bias_grads]).reshape(norm_params.shape)
    step_count = iteration[0].astype(jnp.float32)
    squeeze_out = adamw_step(
        squeeze_weight,
        squeeze_moment,
        squeeze_second,
        slot_squeeze,
        C_IN ** (-0.5),
        DECAY_RATE,
        step_count,
    )
    spatial_out = adamw_step(
        spatial_weight,
        spatial_moment,
        spatial_second,
        slot_spatial,
        (9 * C_MID) ** (-0.5),
        DECAY_RATE,
        step_count,
    )
    expand_out = adamw_step(
        expand_weight,
        expand_moment,
        expand_second,
        slot_expand,
        C_MID ** (-0.5),
        DECAY_RATE,
        step_count,
    )
    hidden_out = adamw_step(
        hidden_weight,
        hidden_moment,
        hidden_second,
        slot_hidden,
        C_IN ** (-0.5),
        DECAY_RATE,
        step_count,
    )
    project_new = adamw_step(
        project_weight,
        project_moment,
        project_second,
        slot_project,
        HID ** (-0.5),
        DECAY_RATE,
        step_count,
    )
    proto_out = adamw_step(
        prototypes, proto_moment, proto_second, proto_grad, 0.1, DECAY_RATE, step_count
    )
    norm_out = adamw_step(
        norm_params, norm_moment, norm_second, norm_gradient, 0.5, 0.0, step_count
    )
    return (
        block_out,
        loss,
        images_grad,
        squeeze_out[0],
        squeeze_out[1],
        squeeze_out[2],
        spatial_out[0],
        spatial_out[1],
        spatial_out[2],
        expand_out[0],
        expand_out[1],
        expand_out[2],
        hidden_out[0],
        hidden_out[1],
        hidden_out[2],
        project_new[0],
        project_new[1],
        project_new[2],
        proto_out[0],
        proto_out[1],
        proto_out[2],
        norm_out[0],
        norm_out[1],
        norm_out[2],
    )


def solution(mesh):
    placed = (
        P("dp", None, None, None),
        P("dp"),
        P(),
        P("dp", "chan"),
        P("dp", "chan"),
        P("dp", "chan"),
        P("dp", "chan"),
        P("dp", "chan"),
        P("dp", "chan"),
        P("dp", "chan"),
        P("dp", "chan"),
        P("dp", "chan"),
        P("dp", "chan"),
        P("dp", "chan"),
        P("dp", "chan"),
        P("dp", None),
        P("dp", None),
        P("dp", None),
        P(),
        P(),
        P(),
        P(None, "chan", None),
        P(None, "chan", None),
        P(None, "chan", None),
        P("dp", None),
        P("dp"),
        P(),
        P(),
    )
    return jax.shard_map(
        local,
        mesh=mesh,
        in_specs=placed,
        out_specs=(
            P("dp", None, None, "chan"),
            P(),
            P("dp", None, None, "chan"),
            P("dp", "chan"),
            P("dp", "chan"),
            P("dp", "chan"),
            P("dp", "chan"),
            P("dp", "chan"),
            P("dp", "chan"),
            P("dp", "chan"),
            P("dp", "chan"),
            P("dp", "chan"),
            P("dp", "chan"),
            P("dp", "chan"),
            P("dp", "chan"),
            P("dp", None),
            P("dp", None),
            P("dp", None),
            P(),
            P(),
            P(),
            P(None, "chan", None),
            P(None, "chan", None),
            P(None, "chan", None),
        ),
        check_vma=False,
    )
```

profile of v0, /device:TPU:0, one launch (start us, length us, event | category | flops | bytes accessed | tf_op | source)
XLA Modules:
  0.0 1566.3 jit_solution(13299392214432998850)
XLA Ops:
  30.9 15.5 scatter_custom_fusion
  66.3 19.3 %all-reduce.13 = (f32[128]{0:T(128)S(1)}, f32[128]{0:T(128)S(1)}) all-reduce(f32[128]{0:T(128)S(1)} %get-tuple-element.431, f32[128]{0:T(128)S(1)} %get-tuple-element.430), channel_id=1, replica_groups=mesh['dp'=8,'chan'=4] {'dp'}, use_global_device_ids=true, to_apply=%region_4.0 | all-reduce | flops 256 | bytes 2048 | tf_op jit(solution)/shard_map/psum | solution.py:35
  102.2 14.0 all-gather.10.cloned.1.call-done
  119.9 10.7 pad_slice_fusion
  179.2 21.4 %all-reduce.12 = (f32[128]{0:T(128)S(1)}, f32[128]{0:T(128)S(1)}) all-reduce(f32[128]{0:T(128)S(1)} %get-tuple-element.429, f32[128]{0:T(128)S(1)} %get-tuple-element.428), channel_id=1, replica_groups=mesh['dp'=8,'chan'=4] {'dp'}, use_global_device_ids=true, to_apply=%region_8.9 | all-reduce | flops 256 | bytes 2048 | tf_op jit(solution)/shard_map/psum | solution.py:35
  221.9 54.6 %all-gather.16.cloned.1.call-done = bf16[4096,512]{1,0:T(8,128)(2,1)} async-done(((bf16[512,512]{1,0:T(8,128)(2,1)}), bf16[4096,512]{1,0:T(8,128)(2,1)}) %all-gather.16.cloned.1.call-update) | async-done | bytes 4194320 | tf_op jit(solution)/shard_map/all_gather | solution.py:135
  276.5 12.0 gather_fusion.2
  288.5 89.7 %reduce-scatter.10.cloned.1.call-done = f32[1568,512]{1,0:T(8,128)} async-done(((f32[1568,2048]{1,0:T(8,128)}), f32[1568,512]{1,0:T(8,128)}) %reduce-scatter.10.cloned.1.call-update) | async-done | bytes 3211280 | tf_op jit(solution)/shard_map/reduce_scatter | solution.py:168
  380.6 21.5 %all-reduce.11 = (f32[512]{0:T(512)S(1)}, f32[512]{0:T(512)S(1)}) all-reduce(f32[512]{0:T(512)S(1)} %get-tuple-element.423, f32[512]{0:T(512)S(1)} %get-tuple-element.422), channel_id=1, replica_groups=mesh['dp'=8,'chan'=4] {'dp'}, use_global_device_ids=true, to_apply=%region_13.14 | all-reduce | flops 1024 | bytes 8192 | tf_op jit(solution)/shard_map/psum | solution.py:35
  421.8 17.1 %all-reduce.10 = (f32[512]{0:T(512)S(1)}, f32[512]{0:T(512)S(1)}) all-reduce(f32[512]{0:T(512)S(1)} %get-tuple-element.441, f32[512]{0:T(512)S(1)} %get-tuple-element.440), channel_id=1, replica_groups=mesh['dp'=8,'chan'=4] {'dp'}, use_global_device_ids=true, to_apply=%region_18.19 | all-reduce | flops 1024 | bytes 8192 | tf_op jit(solution)/shard_map/psum | solution.py:35
  449.7 34.8 %psum.155 = f32[3000]{0:T(1024)S(1)} all-reduce(f32[3000]{0:T(1024)S(1)} %add.431), channel_id=1, replica_groups=mesh['dp'=8,'chan'=4] {'dp'}, use_global_device_ids=true, to_apply=%region_22.23 | all-reduce | flops 3000 | bytes 24000 | tf_op jit(solution)/shard_map/psum | solution.py:201
  492.1 33.0 %psum.156 = f32[3000]{0:T(1024)S(1)} all-reduce(f32[3000]{0:T(1024)S(1)} %add.432), channel_id=1, replica_groups=mesh['dp'=8,'chan'=4] {'dp'}, use_global_device_ids=true, to_apply=%region_27.28 | all-reduce | flops 3000 | bytes 24000 | tf_op jit(solution)/shard_map/psum | solution.py:201
  534.6 33.0 %psum.157 = f32[3000]{0:T(1024)S(1)} all-reduce(f32[3000]{0:T(1024)S(1)} %add.433), channel_id=1, replica_groups=mesh['dp'=8,'chan'=4] {'dp'}, use_global_device_ids=true, to_apply=%region_32.33 | all-reduce | flops 3000 | bytes 24000 | tf_op jit(solution)/shard_map/psum | solution.py:201
  575.0 17.1 %all-reduce.9 = (f32[512]{0:T(512)S(1)}, f32[512]{0:T(512)S(1)}) all-reduce(f32[512]{0:T(512)S(1)} %get-tuple-element.439, f32[512]{0:T(512)S(1)} %get-tuple-element.438), channel_id=1, replica_groups=mesh['dp'=8,'chan'=4] {'dp'}, use_global_device_ids=true, to_apply=%region_44.45 | all-reduce | flops 1024 | bytes 8192 | tf_op jit(solution)/shard_map/psum | solution.py:35
  597.1 17.5 %reduce-scatter.12.cloned.1.call-done = f32[32,512]{1,0:T(8,128)} async-done(((f32[32,2048]{1,0:T(8,128)}), f32[32,512]{1,0:T(8,128)}) %reduce-scatter.12.cloned.1.call-update) | async-done | bytes 65552 | tf_op jit(solution)/shard_map/reduce_scatter | solution.py:240
  625.9 21.3 %all-reduce.8 = (f32[512]{0:T(512)S(1)}, f32[512]{0:T(512)S(1)}) all-reduce(f32[512]{0:T(512)S(1)} %get-tuple-element.421, f32[512]{0:T(512)S(1)} %get-tuple-element.420), channel_id=1, replica_groups=mesh['dp'=8,'chan'=4] {'dp'}, use_global_device_ids=true, to_apply=%region_49.50 | all-reduce | flops 1024 | bytes 8192 | tf_op jit(solution)/shard_map/psum | solution.py:35
  653.4 41.6 %all-gather.20.cloned.1.call-done = bf16[1568,2048]{1,0:T(8,128)(2,1)} async-done(((bf16[1568,512]{1,0:T(8,128)(2,1)}), bf16[1568,2048]{1,0:T(8,128)(2,1)}) %all-gather.20.cloned.1.call-update) | async-done | bytes 6422544 | tf_op jit(solution)/shard_map/all_gather | solution.py:249
  701.0 21.3 %all-reduce.7 = (f32[128]{0:T(128)S(1)}, f32[128]{0:T(128)S(1)}) all-reduce(f32[128]{0:T(128)S(1)} %get-tuple-element.427, f32[128]{0:T(128)S(1)} %get-tuple-element.426), channel_id=1, replica_groups=mesh['dp'=8,'chan'=4] {'dp'}, use_global_device_ids=true, to_apply=%region_53.54 | all-reduce | flops 256 | bytes 2048 | tf_op jit(solution)/shard_map/psum | solution.py:35
  723.8 11.5 fusion.96
  735.3 35.7 %reshape.615 = f32[32,7,7,9,512]{4,3,2,1,0:T(8,128)} reshape(f32[1568,4608]{1,0:T(8,128)} %fusion.96) | data formatting | bytes 57802752 | tf_op jit(solution)/shard_map/reshape | solution.py:67
  771.0 79.0 %fusion.90 = (f32[32,7,7,1,512]{4,3,2,1,0:T(1,128)}, f32[32,7,7,1,512]{4,3,2,1,0:T(1,128)}, f32[32,7,7,1,512]{4,3,2,1,0:T(1,128)}, f32[32,7,7,1,512]{4,3,2,1,0:T...) fusion(f32[32,7,7,9,512]{4,3,2,1,0:T(8,128)} %reshape.615), kind=kLoop, calls=%fused_computation.219 | loop fusion | bytes 57802752 | tf_op jit(solution)/shard_map/slice | solution.py:72
  881.8 14.2 gather_fusion.7
  901.2 14.2 gather_fusion.5
  928.1 20.2 %gather_fusion.6 = f32[4096,512]{1,0:T(8,128)} fusion(f32[2049,512]{1,0:T(8,128)} %concatenate.93, s32[4096]{0:T(1024)S(1)} %copy-done.43), kind=kCustom, calls=%fused_computation.6 | custom fusion | bytes 16793600 | tf_op jit(solution)/shard_map/gather | solution.py:279
  951.1 18.7 %all-reduce.6 = (f32[1]{0:T(128)}, f32[128]{0:T(128)S(1)}, f32[128]{0:T(128)S(1)}) all-reduce(f32[1]{0:T(128)} %bitcast.10, f32[128]{0:T(128)S(1)} %get-tuple-element.425, f32[128]{0:T(128)S(1)} %get-tuple-element.424), channel_id=1, replica_groups=mesh['dp'=8,'chan'=4] {'dp'}, use_global_device_ids=true, to_apply=%region_38.39 | all-reduce | flops 257 | bytes 2056 | tf_op jit(solution)/shard_map/psum | solution.py:225
  974.5 14.2 gather_fusion.4
  1012.2 65.1 %reduce-scatter.26.cloned.1.call-done = f32[512,128]{1,0:T(8,128)} async-done(((f32[4096,128]{1,0:T(8,128)}), f32[512,128]{1,0:T(8,128)}) %reduce-scatter.26.cloned.1.call-update) | async-done | bytes 262160 | tf_op jit(solution)/shard_map/reduce_scatter | solution.py:280
  1079.2 68.4 %reduce-scatter.22.cloned.1.call-done = f32[512,128]{1,0:T(8,128)} async-done(((f32[4096,128]{1,0:T(8,128)}), f32[512,128]{1,0:T(8,128)}) %reduce-scatter.22.cloned.1.call-update) | async-done | bytes 262160 | tf_op jit(solution)/shard_map/reduce_scatter | solution.py:278
  1149.5 69.4 %reduce-scatter.20.cloned.1.call-done = f32[576,128]{1,0:T(8,128)} async-done(((f32[4608,128]{1,0:T(8,128)}), f32[576,128]{1,0:T(8,128)}) %reduce-scatter.20.cloned.1.call-update) | async-done | bytes 294928 | tf_op jit(solution)/shard_map/reduce_scatter | solution.py:281
  1222.4 148.1 %reduce-scatter.24.cloned.1.call-done = f32[512,512]{1,0:T(8,128)} async-done(((f32[4096,512]{1,0:T(8,128)}), f32[512,512]{1,0:T(8,128)}) %reduce-scatter.24.cloned.1.call-update) | async-done | bytes 1048592 | tf_op jit(solution)/shard_map/reduce_scatter | solution.py:279
  1374.9 66.3 %reduce-scatter.18.cloned.1.call-done = f32[512,128]{1,0:T(8,128)} async-done(((f32[4096,128]{1,0:T(8,128)}), f32[512,128]{1,0:T(8,128)}) %reduce-scatter.18.cloned.1.call-update) | async-done | bytes 262160 | tf_op jit(solution)/shard_map/reduce_scatter | solution.py:277
  1443.3 100.3 %reduce-scatter.16.cloned.1.call-done = f32[1568,512]{1,0:T(8,128)} async-done(((f32[1568,2048]{1,0:T(8,128)}), f32[1568,512]{1,0:T(8,128)}) %reduce-scatter.16.cloned.1.call-update) | async-done | bytes 3211280 | tf_op jit(solution)/shard_map/reduce_scatter | solution.py:270
  (373 shorter events, 325.9 us)
Async XLA Ops:
  7.2 201.5 %copy-start = (bf16[480,128]{1,0:T(8,128)(2,1)S(1)}, bf16[480,128]{1,0:T(8,128)(2,1)}, u32[]{:S(2)}) copy-start(bf16[480,128]{1,0:T(8,128)(2,1)} %param.70) | copy-start | bytes 368644
  7.2 46.4 %all-gather.8.cloned.1.call-start = ((), (), s32[]{:S(2)}) async-start(), calls=%async_computation.9 | async-start | bytes 1179648 | tf_op jit(solution)/shard_map/all_gather | solution.py:133
  8.9 86.4 %all-gather.14.cloned.1.call-start = ((), (), s32[]{:S(2)}) async-start(), calls=%async_computation.12 | async-start | bytes 1179648 | tf_op jit(solution)/shard_map/all_gather | solution.py:134
  10.6 105.7 %all-gather.10.cloned.1.call-start = ((), (), s32[]{:S(2)}) async-start(), calls=%async_computation.10 | async-start | bytes 2007040 | tf_op jit(solution)/shard_map/all_gather | solution.py:160
  87.2 84.4 %all-gather.12.cloned.1.call-start = ((), (), s32[]{:S(2)}) async-start(), calls=%async_computation.11 | async-start | bytes 1327104 | tf_op jit(solution)/shard_map/all_gather | solution.py:137
  88.0 124.8 %all-gather.18.cloned.1.call-start = ((), (), s32[]{:S(2)}) async-start(), calls=%async_computation.15 | async-start | bytes 1179648 | tf_op jit(solution)/shard_map/all_gather | solution.py:136
  88.7 187.7 %all-gather.16.cloned.1.call-start = ((), (), s32[]{:S(2)}) async-start(), calls=%async_computation.14 | async-start | bytes 4718592 | tf_op jit(solution)/shard_map/all_gather | solution.py:135
  89.7 288.5 %reduce-scatter.10.cloned.1.call-start = ((), (), s32[]{:S(2)}) async-start(), calls=%async_computation.13 | async-start | bytes 16056320 | tf_op jit(solution)/shard_map/reduce_scatter | solution.py:168
  207.7 407.0 %reduce-scatter.12.cloned.1.call-start = ((), (), s32[]{:S(2)}) async-start(), calls=%async_computation.16 | async-start | bytes 327680 | tf_op jit(solution)/shard_map/reduce_scatter | solution.py:240
  209.0 230.5 %copy-start.67 = (f32[1,512]{1,0:T(1,128)}, f32[1,512]{1,0:T(1,128)S(1)}, u32[]{:S(2)}) copy-start(f32[1,512]{1,0:T(1,128)S(1)} %get-tuple-element.508) | copy-start | bytes 6148
  596.6 98.4 %all-gather.20.cloned.1.call-start = ((), (), s32[]{:S(2)}) async-start(), calls=%async_computation.17 | async-start | bytes 8028160 | tf_op jit(solution)/shard_map/all_gather | solution.py:249
  651.4 297.7 %reduce-scatter.14.cloned.1.call-start = ((), (), s32[]{:S(2)}) async-start(), calls=%async_computation.18 | async-start | bytes 4014080 | tf_op jit(solution)/shard_map/reduce_scatter | solution.py:261
  879.0 127.6 %all-reduce.16.cloned.1.call-start = ((), (), s32[]{:S(2)}) async-start(), calls=%async_computation.25 | async-start | bytes 3072000 | tf_op jit(solution)/shard_map/psum | solution.py:225
  881.3 195.9 %reduce-scatter.26.cloned.1.call-start = ((), (), s32[]{:S(2)}) async-start(), calls=%async_computation.24 | async-start | bytes 2359296 | tf_op jit(solution)/shard_map/reduce_scatter | solution.py:280
  896.0 251.6 %reduce-scatter.22.cloned.1.call-start = ((), (), s32[]{:S(2)}) async-start(), calls=%async_computation.22 | async-start | bytes 2359296 | tf_op jit(solution)/shard_map/reduce_scatter | solution.py:278
  915.5 303.5 %reduce-scatter.20.cloned.1.call-start = ((), (), s32[]{:S(2)}) async-start(), calls=%async_computation.21 | async-start | bytes 2654208 | tf_op jit(solution)/shard_map/reduce_scatter | solution.py:281
  924.9 445.6 %reduce-scatter.24.cloned.1.call-start = ((), (), s32[]{:S(2)}) async-start(), calls=%async_computation.23 | async-start | bytes 9437184 | tf_op jit(solution)/shard_map/reduce_scatter | solution.py:279
  948.4 492.8 %reduce-scatter.18.cloned.1.call-start = ((), (), s32[]{:S(2)}) async-start(), calls=%async_computation.20 | async-start | bytes 2359296 | tf_op jit(solution)/shard_map/reduce_scatter | solution.py:277
  988.7 554.9 %reduce-scatter.16.cloned.1.call-start = ((), (), s32[]{:S(2)}) async-start(), calls=%async_computation.19 | async-start | bytes 16056320 | tf_op jit(solution)/shard_map/reduce_scatter | solution.py:270
  1012.1 206.9 %copy-start.35 = (f32[576,128]{1,0:T(8,128)S(1)}, f32[576,128]{1,0:T(8,128)}, u32[]{:S(2)}) copy-start(f32[576,128]{1,0:T(8,128)} %param.52) | copy-start | bytes 884740
  1012.1 206.9 %copy-start.46 = (f32[576,128]{1,0:T(8,128)S(1)}, f32[576,128]{1,0:T(8,128)}, u32[]{:S(2)}) copy-start(f32[576,128]{1,0:T(8,128)} %param.54) | copy-start | bytes 884740
  1012.1 206.9 %copy-start.47 = (f32[576,128]{1,0:T(8,128)S(1)}, f32[576,128]{1,0:T(8,128)}, u32[]{:S(2)}) copy-start(f32[576,128]{1,0:T(8,128)} %param.53) | copy-start | bytes 884740
  1012.1 209.5 %copy-start.63 = (f32[512]{0:T(512)S(1)}, f32[512]{0:T(512)}, u32[]{:S(2)}) copy-start(f32[512]{0:T(512)} %copy-done.62) | copy-start | bytes 6148
  1012.1 209.5 %copy-start.65 = (f32[512]{0:T(512)S(1)}, f32[512]{0:T(512)}, u32[]{:S(2)}) copy-start(f32[512]{0:T(512)} %copy-done.64) | copy-start | bytes 6148
  1012.1 209.5 %copy-start.79 = (f32[512]{0:T(512)S(1)}, f32[512]{0:T(512)}, u32[]{:S(2)}) copy-start(f32[512]{0:T(512)} %copy-done.78) | copy-start | bytes 6148
  1012.1 209.5 %copy-start.81 = (f32[512]{0:T(512)S(1)}, f32[512]{0:T(512)}, u32[]{:S(2)}) copy-start(f32[512]{0:T(512)} %copy-done.80) | copy-start | bytes 6148
  1012.1 209.5 %copy-start.93 = (f32[128]{0:T(128)S(1)}, f32[128]{0:T(128)}, u32[]{:S(2)}) copy-start(f32[128]{0:T(128)} %copy-done.92) | copy-start | bytes 1540
  1012.1 209.5 %copy-start.95 = (f32[128]{0:T(128)S(1)}, f32[128]{0:T(128)}, u32[]{:S(2)}) copy-start(f32[128]{0:T(128)} %copy-done.94) | copy-start | bytes 1540
  1012.1 209.6 %copy-start.52 = (f32[2,1,1280]{2,1,0:T(1,128)S(1)}, f32[2,1,1280]{2,1,0:T(1,128)}, u32[]{:S(2)}) copy-start(f32[2,1,1280]{2,1,0:T(1,128)} %param.67) | copy-start | bytes 30724
  1012.1 209.6 %copy-start.56 = (f32[2,1,1280]{2,1,0:T(1,128)S(1)}, f32[2,1,1280]{2,1,0:T(1,128)}, u32[]{:S(2)}) copy-start(f32[2,1,1280]{2,1,0:T(1,128)} %param.69) | copy-start | bytes 30724
  1012.2 209.6 %copy-start.57 = (f32[2,1,1280]{2,1,0:T(1,128)S(1)}, f32[2,1,1280]{2,1,0:T(1,128)}, u32[]{:S(2)}) copy-start(f32[2,1,1280]{2,1,0:T(1,128)} %param.68) | copy-start | bytes 30724
  1222.4 321.2 %copy-start.3 = (f32[1568,512]{1,0:T(8,128)S(1)}, f32[1568,512]{1,0:T(8,128)}, u32[]{:S(2)}) copy-start(f32[1568,512]{1,0:T(8,128)} %get-tuple-element.481) | copy-start | bytes 9633796
  (84 other events, 2199.3 us)
Sparse Core Ops, SparseCore 0:
  10.7 42.8 all-gather.7
  56.3 38.8 all-gather.13
  97.4 18.8 all-gather.9
  118.9 41.0 all-gather.11
  162.5 39.1 all-gather.17
  204.2 72.2 all-gather.15
  279.1 99.0 reduce-scatter.9
  596.7 17.8 reduce-scatter.11
  651.6 43.4 all-gather.19
  879.1 34.6 reduce-scatter.13
  917.9 88.6 all-reduce.15
  1010.0 67.1 reduce-scatter.25
  1080.8 66.7 reduce-scatter.21
  1150.9 67.9 reduce-scatter.19
  1222.4 148.0 reduce-scatter.23
  1374.3 66.8 reduce-scatter.17
  1443.8 99.7 reduce-scatter.15
where the time goes:
time: 1580 us; the launch traced here: 1570 us
  waiting for transfers between devices  754 us (48%)
  local copies, waits for them, and re-layouts  353 us (22%)
  blocking collectives  270 us (17%)
  other arithmetic  86.8 us (5%)
  matrix products  81.7 us (5%)
  between operations  19.5 us (1%)
    reduce_scatter x1, waiting for transfers between devices, local(): lax.psum_scatter(pad_rows(hidden_grad)[slot_rows], 'dp', scatter_dimensio...  148 us
    psum x7, blocking collectives, image_sums(): return lax.psum((first_term, second_term), 'dp')  139 us
    psum x3, blocking collectives, local(): lax.psum(jnp.sum(batch_codes, axis=0) + jnp.sum(queue_codes, axis=0), 'dp')  101 us
    reduce_scatter x1, waiting for transfers between devices, local(): lax.psum_scatter(input_terms, 'chan', scatter_dimension=1, tiled=True)  100 us
    reduce_scatter x1, waiting for transfers between devices, local(): lax.psum_scatter(expand_terms, 'chan', scatter_dimension=1, tiled=True)  89.7 us
    slice x2, local copies, waits for them, and re-layouts, patch_back(): tap_grads[:, :, :, row_at * 3 + col_at, :]  81.4 us
    reduce_scatter x1, waiting for transfers between devices, local(): lax.psum_scatter(spatial_grad, 'dp', scatter_dimension=0, tiled=True)  69.4 us
    reduce_scatter x1, waiting for transfers between devices, local(): lax.psum_scatter(pad_rows(expand_grad)[slot_rows], 'dp', scatter_dimensio...  68.4 us
  transfers between devices with their start and end apart: 17, of which 14 were waited for; matrix products, arithmetic and copies ran while one was open for 18% of the time, Pallas kernels for 0%

commit v1 on v0

v1 whole, which is shorter than its diff:
```python
import jax
import jax.numpy as jnp
from jax import lax
from jax.sharding import PartitionSpec as P

SINK_ITERS = 3
PRECISE = lax.Precision.HIGHEST
EPS_SINK = 0.05
SOFTMAX_WARMTH = 0.1
LOSS_MULTIPLIER = 256.0
NORM_EPS = 1e-05
BETA_ONE = 0.5
BETA_TWO = 0.5
ADAM_EPS = 1e-08
DECAY_RATE = 1e-06
LOW = jnp.bfloat16
WIDE = jnp.float32


def contract(left, right, left_dim, right_dim):
    return lax.dot_general(
        left, right, (((left_dim,), (right_dim,)), ((), ())), preferred_element_type=WIDE
    )


def silu_slope(value):
    sigma = jax.nn.sigmoid(value)
    return sigma * (1.0 + value * (1.0 - sigma))


def spread(value, axis):
    count = lax.axis_size(axis)
    return lax.all_to_all(jnp.broadcast_to(value[None], (count,) + value.shape), axis, 0, 0)


def total(value, axis):
    return jnp.sum(spread(value, axis).astype(WIDE), axis=0)


def swap(value, axis, bit):
    return lax.ppermute(value, axis, [(at, at ^ bit) for at in range(lax.axis_size(axis))])


def gather_relative(value, axis):
    held = {0: value}
    bit = lax.axis_size(axis) // 2
    while bit:
        keys = sorted(held)
        came = swap(jnp.stack([held[k] for k in keys]), axis, bit)
        held.update({k ^ bit: came[n] for n, k in enumerate(keys)})
        bit //= 2
    return [held[k] for k in range(lax.axis_size(axis))]


def scatter_relative(parts, axis, sent=LOW):
    held = dict(enumerate(parts))
    bit = 1
    while bit < lax.axis_size(axis):
        keys = [k for k in sorted(held) if not k & bit]
        came = swap(jnp.stack([held[k | bit].astype(sent) for k in keys]), axis, bit)
        held = {k: held[k] + came[n].astype(WIDE) for n, k in enumerate(keys)}
        bit *= 2
    return held[0]


def total_hyper(value, axis):
    bit = 1
    while bit < lax.axis_size(axis):
        value = value + swap(value, axis, bit)
        bit *= 2
    return value


def block_at(value, index, size, dim):
    return lax.dynamic_slice_in_dim(value, index * size, size, dim)


def statistics(sums, row_total):
    average = sums[0] / row_total
    variance = sums[1] / row_total - average * average
    return average, lax.rsqrt(variance + NORM_EPS)


def backward_of_norm(grad_out, centred, inv_std, gain_row, sums, row_total):
    return gain_row * inv_std * (grad_out - (sums[0] + centred * sums[1]) / row_total)


def adamw_step(weight, moment_one, moment_two, gradient, learn_rate, weight_decay, step_count):
    moment_new = BETA_ONE * moment_one + (1.0 - BETA_ONE) * gradient
    second_new = BETA_TWO * moment_two + (1.0 - BETA_TWO) * gradient * gradient
    fix_one = 1.0 - jnp.power(BETA_ONE, step_count)
    fix_two = 1.0 - jnp.power(BETA_TWO, step_count)
    update = moment_new / fix_one / (jnp.sqrt(second_new / fix_two) + ADAM_EPS)
    return (weight - learn_rate * (update + weight_decay * weight), moment_new, second_new)


def local(
    images,
    crop_image,
    slot_rows,
    squeeze_weight,
    squeeze_moment,
    squeeze_second,
    spatial_weight,
    spatial_moment,
    spatial_second,
    expand_weight,
    expand_moment,
    expand_second,
    hidden_weight,
    hidden_moment,
    hidden_second,
    project_weight,
    project_moment,
    project_second,
    prototypes,
    proto_moment,
    proto_second,
    norm_params,
    norm_moment,
    norm_second,
    queue_rows,
    queue_valid,
    queue_fill,
    iteration,
):
    dp_count = lax.axis_size("dp")
    dp_at = lax.axis_index("dp")
    chan_count = lax.axis_size("chan")
    chan_at = lax.axis_index("chan")
    crops_dev, map_side, _, in_width = images.shape
    map_area = map_side * map_side
    pixel_rows = crops_dev * map_area
    pixel_total = pixel_rows * dp_count
    crop_total = crops_dev * dp_count
    mid_local = squeeze_weight.shape[1]
    hid_local = hidden_weight.shape[1]
    out_local = in_width // chan_count
    slot_local = squeeze_weight.shape[0]
    slot_total = slot_rows.shape[0]
    mid_width = mid_local * chan_count
    hid_width = hid_local * chan_count

    channels = jnp.arange(in_width, dtype=jnp.int32)
    place_hot = (slot_rows[None, :] == channels[:, None]).astype(LOW)
    own_slots = block_at(slot_rows, dp_at, slot_local, 0)
    own_hot = (own_slots[:, None] == channels[None, :]).astype(LOW)
    slot_hot = (slot_rows[:, None] == channels[None, :]).astype(LOW)
    slot_hot_rel = (
        (slot_rows ^ (chan_at * out_local))[:, None] == channels[None, :]
    ).astype(LOW)

    squeeze_all = spread(squeeze_weight.astype(LOW), "dp").reshape(slot_total, mid_local)
    spatial_all = lax.all_gather(spatial_weight.astype(LOW), "dp", axis=0, tiled=True)
    expand_all = lax.all_gather(expand_weight.astype(LOW), "dp", axis=0, tiled=True)
    head_all = lax.all_gather(
        jnp.concatenate([hidden_weight.astype(LOW), project_weight.astype(LOW)], axis=1),
        "dp",
        axis=0,
        tiled=True,
    )
    squeeze_rows = contract(place_hot, squeeze_all, 1, 0).astype(LOW)

    norm_rows = norm_params[:, 0, :]
    first_norm = norm_rows[:, :mid_local]
    second_norm = norm_rows[:, mid_local : 2 * mid_local]
    third_norm = norm_rows[:, 2 * mid_local : 2 * mid_local + out_local]
    head_norm = norm_rows[:, 2 * mid_local + out_local :]

    def inner_layer(pre_act, norm):
        sums = jnp.stack([jnp.sum(pre_act, axis=0), jnp.sum(pre_act * pre_act, axis=0)])
        raw_all = jnp.concatenate(gather_relative(pre_act.astype(LOW), "chan"), axis=1)
        average, inv_std = statistics(total(sums, "dp"), pixel_total)
        scale = inv_std * norm[0]
        affine = jnp.stack([scale, norm[1] - average * scale])
        affine_all = jnp.concatenate(gather_relative(affine, "chan"), axis=1)
        act_all = jax.nn.silu(raw_all.astype(WIDE) * affine_all[0] + affine_all[1]).astype(LOW)
        return act_all, average, inv_std

    pixels = images.transpose(1, 2, 0, 3).reshape(pixel_rows, in_width)
    pre_one = contract(pixels, squeeze_rows, 1, 0)
    inner_one, average_one, inv_one = inner_layer(pre_one, first_norm)

    def relative_blocks(value, size, dim):
        return [block_at(value, chan_at ^ r, size, dim) for r in range(chan_count)]

    spatial_rel = jnp.concatenate(
        relative_blocks(spatial_all.reshape(9, mid_width, mid_local), mid_local, 1), axis=1
    ).reshape(3, 3, mid_width, mid_local)
    maps_one = inner_one.reshape(map_side, map_side, crops_dev, mid_width)
    conv_dims = lax.ConvDimensionNumbers((2, 3, 0, 1), (3, 2, 0, 1), (2, 3, 0, 1))
    pre_two = lax.conv_general_dilated(
        maps_one,
        spatial_rel,
        (1, 1),
        ((1, 1), (1, 1)),
        dimension_numbers=conv_dims,
        preferred_element_type=WIDE,
    ).reshape(pixel_rows, mid_local)
    inner_two, average_two, inv_two = inner_layer(pre_two, second_norm)

    expand_rows = contract(place_hot, expand_all, 1, 0).astype(LOW)
    expand_sent = relative_blocks(expand_rows, out_local, 0)
    expand_rel = jnp.concatenate(
        [expand_sent[0]] + [swap(expand_sent[r], "chan", r) for r in range(1, chan_count)], axis=1
    )
    squeeze_sent = relative_blocks(squeeze_rows, out_local, 0)
    squeeze_rel = jnp.concatenate(
        [squeeze_sent[0]] + [swap(squeeze_sent[r], "chan", r) for r in range(1, chan_count)],
        axis=1,
    )
    pre_three = contract(inner_two, expand_rel, 1, 1)
    sums_three = total(
        jnp.stack([jnp.sum(pre_three, axis=0), jnp.sum(pre_three * pre_three, axis=0)]), "dp"
    )
    average_three, inv_three = statistics(sums_three, pixel_total)
    centred_three = (pre_three - average_three) * inv_three
    residual_in = block_at(pixels, chan_at, out_local, 1).astype(WIDE)
    summed = centred_three * third_norm[0] + third_norm[1] + residual_in
    block_rows = jax.nn.silu(summed)
    block_out = block_rows.astype(LOW).reshape(map_side, map_side, crops_dev, out_local)
    block_out = block_out.transpose(2, 0, 1, 3)
    pooled = jnp.mean(block_rows.reshape(map_area, crops_dev, out_local), axis=0).astype(LOW)
    pooled_dev = lax.all_gather(pooled, "chan", axis=1, tiled=True)
    pooled_all = lax.all_gather(pooled_dev, "dp", axis=0, tiled=True)

    hidden_rows = contract(place_hot, head_all[:, :hid_local], 1, 0).astype(LOW)
    project_rows = contract(
        block_at(place_hot, chan_at, hid_local, 0), head_all[:, hid_local:], 1, 0
    ).astype(LOW)
    hidden_dev = contract(pooled_dev, hidden_rows, 1, 0)
    hidden_pre = spread(hidden_dev.astype(LOW), "dp").reshape(crop_total, hid_local).astype(WIDE)
    head_sums = jnp.stack([jnp.sum(hidden_pre, axis=0), jnp.sum(hidden_pre * hidden_pre, axis=0)])
    average_head, inv_head = statistics(head_sums, crop_total)
    centred_head = (hidden_pre - average_head) * inv_head
    normed_head = centred_head * head_norm[0] + head_norm[1]
    hidden_act = jax.nn.silu(normed_head).astype(LOW)
    project_out = total_hyper(contract(hidden_act, project_rows, 1, 0), "chan")
    inv_len = lax.rsqrt(jnp.sum(project_out * project_out, axis=1, keepdims=True) + 1e-06)
    normed = project_out * inv_len
    normed_low = normed.astype(LOW)
    proto_low = prototypes.astype(LOW).T
    proto_count = proto_low.shape[0]
    prototype_scores = contract(normed_low, proto_low, 1, 1)
    queue_similarity = contract(queue_rows, proto_low, 1, 1)
    queue_len = queue_rows.shape[0]
    slot_index = dp_at * queue_len + jnp.arange(queue_len, dtype=jnp.int32)
    queue_live = (queue_valid > 0) & (slot_index < queue_fill[0])
    queue_codes = jnp.exp(queue_similarity / EPS_SINK) * queue_live[:, None].astype(WIDE)
    queue_first = spread(
        jnp.concatenate([jnp.sum(queue_codes, axis=0), crop_image.astype(WIDE)]), "dp"
    )
    labels = queue_first[:, proto_count:].reshape(crop_total)

    batch_codes = jnp.exp(prototype_scores / EPS_SINK)
    proto_totals = jnp.sum(batch_codes, axis=0) + jnp.sum(queue_first[:, :proto_count], axis=0)

    def live_inverse(row_sums):
        return 1.0 / jnp.where(queue_live[:, None], row_sums, 1.0)

    batch_codes = batch_codes / proto_totals
    queue_codes = queue_codes / proto_totals
    batch_codes = batch_codes / jnp.sum(batch_codes, axis=1, keepdims=True)
    queue_codes = queue_codes * live_inverse(jnp.sum(queue_codes, axis=1, keepdims=True))
    batch_scale = 1.0
    queue_scale = 1.0
    for turn_index in range(1, SINK_ITERS):
        column = 1.0 / (
            jnp.sum(batch_codes * batch_scale, axis=0)
            + total(jnp.sum(queue_codes * queue_scale, axis=0), "dp")
        )
        batch_scale = 1.0 / jnp.sum(batch_codes * column, axis=1, keepdims=True)
        queue_scale = live_inverse(jnp.sum(queue_codes * column, axis=1, keepdims=True))
    codes = batch_codes * column * batch_scale

    crop_index = jnp.arange(crop_total, dtype=jnp.int32)
    same_image = (
        (labels[:, None] == labels[None, :])
        & (crop_index[:, None] != crop_index[None, :])
        & (crop_index[:, None] // crops_dev == crop_index[None, :] // crops_dev)
    )
    others = jnp.sum(same_image.astype(WIDE), axis=1, keepdims=True)
    pair_low = same_image.astype(LOW)
    codes_high = codes.astype(LOW)
    codes_rest = (codes - codes_high.astype(WIDE)).astype(LOW)
    target_rows = (
        contract(pair_low, codes_high, 1, 0) + contract(pair_low, codes_rest, 1, 0)
    ) / jnp.maximum(others, 1.0)
    raw_scores = prototype_scores / SOFTMAX_WARMTH
    log_norm = jax.nn.logsumexp(raw_scores, axis=1, keepdims=True)
    log_likelihoods = raw_scores - log_norm
    per_crop = -jnp.sum(target_rows * log_likelihoods, axis=1)
    target_weight_total = jnp.sum(target_rows, axis=1, keepdims=True)
    score_gradient = (
        LOSS_MULTIPLIER
        / SOFTMAX_WARMTH
        * (jnp.exp(log_likelihoods) * target_weight_total - target_rows)
    ).astype(LOW)
    loss = (jnp.sum(per_crop) / crop_total).reshape(1)
    proto_grad = contract(score_gradient, normed_low, 0, 0).T
    normed_grad = contract(score_gradient, proto_low, 1, 0)
    project_low_grad = (
        inv_len * (normed_grad - normed * jnp.sum(normed * normed_grad, axis=1, keepdims=True))
    ).astype(LOW)
    project_grad = lax.all_gather(
        contract(hidden_act, project_low_grad, 0, 0).astype(LOW), "chan", axis=0, tiled=True
    )
    hidden_grad_act = contract(project_low_grad, project_rows, 1, 1) * silu_slope(normed_head)
    head_grads = jnp.stack(
        [jnp.sum(hidden_grad_act, axis=0), jnp.sum(hidden_grad_act * centred_head, axis=0)]
    )
    head_pre_low = backward_of_norm(
        hidden_grad_act, centred_head, inv_head, head_norm[0], head_grads, crop_total
    ).astype(LOW)
    pooled_terms = contract(block_at(head_pre_low, dp_at, crops_dev, 0), hidden_rows, 1, 1)
    pooled_grad = scatter_relative(relative_blocks(pooled_terms, out_local, 1), "chan", WIDE)

    spread_grad = jnp.broadcast_to(
        pooled_grad[None] / map_area, (map_area, crops_dev, out_local)
    ).reshape(pixel_rows, out_local)
    sum_grad = spread_grad * silu_slope(summed)
    third_grads = total(
        jnp.stack([jnp.sum(sum_grad, axis=0), jnp.sum(sum_grad * centred_three, axis=0)]), "dp"
    )
    third_low = backward_of_norm(
        sum_grad, centred_three, inv_three, third_norm[0], third_grads, pixel_total
    ).astype(LOW)

    def inner_backward(terms, pre_act, average, inv_std, norm):
        parts = [terms[:, r * mid_local : (r + 1) * mid_local] for r in range(chan_count)]
        centred = (pre_act - average) * inv_std
        grad = scatter_relative(parts, "chan") * silu_slope(centred * norm[0] + norm[1])
        sums = total(jnp.stack([jnp.sum(grad, axis=0), jnp.sum(grad * centred, axis=0)]), "dp")
        return backward_of_norm(grad, centred, inv_std, norm[0], sums, pixel_total).astype(LOW), sums

    second_low, second_grads = inner_backward(
        contract(third_low, expand_rel, 1, 0), pre_two, average_two, inv_two, second_norm
    )
    expand_terms = contract(third_low, inner_two, 0, 0).astype(LOW)
    expand_parts = [expand_terms[:, r * mid_local : (r + 1) * mid_local] for r in range(chan_count)]
    expand_grad = jnp.concatenate(
        [expand_parts[0]] + [swap(expand_parts[r], "chan", r) for r in range(1, chan_count)], axis=0
    )
    slot_expand = lax.psum_scatter(
        contract(slot_hot_rel, expand_grad, 1, 0).astype(LOW), "dp", scatter_dimension=0, tiled=True
    ).astype(WIDE)

    maps_two = second_low.reshape(map_side, map_side, crops_dev, mid_local)
    first_terms = lax.conv_general_dilated(
        maps_two,
        spatial_rel[::-1, ::-1].transpose(0, 1, 3, 2),
        (1, 1),
        ((1, 1), (1, 1)),
        dimension_numbers=conv_dims,
        preferred_element_type=WIDE,
    ).reshape(pixel_rows, mid_width)
    spatial_terms = lax.conv_general_dilated(
        maps_one,
        maps_two,
        (1, 1),
        ((1, 1), (1, 1)),
        dimension_numbers=lax.ConvDimensionNumbers((3, 2, 0, 1), (3, 2, 0, 1), (2, 3, 0, 1)),
        preferred_element_type=WIDE,
    ).reshape(9, mid_width, mid_local)
    spatial_grad = jnp.concatenate(relative_blocks(spatial_terms.astype(LOW), mid_local, 1), axis=1)
    slot_spatial = jnp.sum(
        lax.all_to_all(
            spatial_grad.reshape(dp_count, -1, mid_local), "dp", 0, 0
        ).astype(WIDE),
        axis=0,
    )
    first_low, first_grads = inner_backward(
        first_terms, pre_one, average_one, inv_one, first_norm
    )
    first_all = jnp.concatenate(gather_relative(first_low, "chan"), axis=1)
    images_grad = contract(first_all, squeeze_rel, 1, 1) + sum_grad
    images_grad = images_grad.reshape(map_side, map_side, crops_dev, out_local).transpose(2, 0, 1, 3)
    squeeze_grad = contract(pixels, first_low, 0, 0).astype(LOW)
    slot_squeeze = jnp.sum(
        lax.all_to_all(
            contract(slot_hot, squeeze_grad, 1, 0).astype(LOW).reshape(dp_count, slot_local, mid_local),
            "dp",
            0,
            0,
        ).astype(WIDE),
        axis=0,
    )
    slot_project = contract(own_hot, project_grad, 1, 0)
    slot_hidden = contract(contract(pooled_all, own_hot, 1, 1).astype(LOW), head_pre_low, 0, 0)

    norm_gradient = jnp.concatenate([first_grads, second_grads, third_grads, head_grads], axis=1)
    norm_gradient = norm_gradient[::-1].reshape(norm_params.shape)
    step_count = iteration[0].astype(WIDE)

    def step(weight, moment, second, gradient, rate, decay=DECAY_RATE):
        return adamw_step(weight, moment, second, gradient, rate, decay, step_count)

    return (
        block_out,
        loss,
        images_grad,
        *step(squeeze_weight, squeeze_moment, squeeze_second, slot_squeeze, in_width ** (-0.5)),
        *step(
            spatial_weight, spatial_moment, spatial_second, slot_spatial, (9 * mid_width) ** (-0.5)
        ),
        *step(expand_weight, expand_moment, expand_second, slot_expand, mid_width ** (-0.5)),
        *step(hidden_weight, hidden_moment, hidden_second, slot_hidden, in_width ** (-0.5)),
        *step(project_weight, project_moment, project_second, slot_project, hid_width ** (-0.5)),
        *step(prototypes, proto_moment, proto_second, proto_grad, 0.1),
        *step(norm_params, norm_moment, norm_second, norm_gradient, 0.5, 0.0),
    )


def solution(mesh):
    rows, both, whole = P("dp", None), P("dp", "chan"), P()
    maps = P("dp", None, None, "chan")
    norm = P(None, "chan", None)
    placed = (
        (P("dp", None, None, None), P("dp"), whole)
        + (both,) * 12
        + (rows,) * 3
        + (whole,) * 3
        + (norm,) * 3
        + (rows, P("dp"), whole, whole)
    )
    return jax.shard_map(
        local,
        mesh=mesh,
        in_specs=placed,
        out_specs=(maps, whole, maps) + (both,) * 12 + (rows,) * 3 + (whole,) * 3 + (norm,) * 3,
        check_vma=False,
    )
```

time: 1580 us -> 506 us (0.32)
  waiting for transfers between devices: 754 us -> 195 us
  local copies, waits for them, and re-layouts: 353 us -> 23.4 us
  blocking collectives: 270 us -> 13.3 us
  starting transfers between devices: 1.75 us -> 76.3 us
  matrix products: 81.7 us -> 99.4 us
    reduce_scatter x9 -> x1, waiting for transfers between devices: 625 us -> 38.6 us  [local(): lax.psum_scatter(contract(slot_hot_rel, expand_grad, 1, 0).astype(LOW), '...]
    psum x11 -> x0, blocking collectives: 259 us -> none  [the longest x7 139 us: image_sums(): return lax.psum((first_term, second_term), 'dp')]
    gather x8 -> x0, local copies, waits for them, and re-layouts: 97.8 us -> none  [the longest x1 20.2 us: local(): pad_rows(hidden_grad)[slot_rows]]
    slice x6, local copies, waits for them, and re-layouts: 96.1 us -> 0.94 us  [the longest x1 0.79 us: local(): expand_terms[:, r * mid_local:(r + 1) * mid_local]]
    all_to_all x0 -> x13, waiting for transfers between devices: none -> 94 us  [the longest x11 64.5 us: spread(): lax.all_to_all(jnp.broadcast_to(value[None], (count,) + value.shape), axi...]
    all_gather x7 -> x4, waiting for transfers between devices: 123 us -> 35.4 us  [the longest x1 35.4 us: local(): lax.all_gather(jnp.concatenate([hidden_weight.astype(LOW), project_weight...]
    reshape x8 -> x0, local copies, waits for them, and re-layouts: 67.7 us -> none  [the longest x1 35.7 us: patch_back(): tap_grads = column_grad.reshape(crops_dev, map_side, map_side, 9, width)]
    all_to_all x0 -> x13, starting transfers between devices: none -> 55.4 us  [the longest x11 48.2 us: spread(): lax.all_to_all(jnp.broadcast_to(value[None], (count,) + value.shape), axi...]
  transfers between devices with their start and end apart: 17 -> 45, of which waited for: 14 -> 20; matrix products, arithmetic and copies ran while one was open for 18% -> 34% of each run, Pallas kernels for 0% -> 0%
where the time goes in v1:
time: 506 us; the launch traced here: 497 us
  waiting for transfers between devices  195 us (39%)
  matrix products  99.4 us (20%)
  starting transfers between devices  76.3 us (15%)
  other arithmetic  71.2 us (14%)
  local copies, waits for them, and re-layouts  23.4 us (5%)
  between operations  19 us (4%)
  blocking collectives  13.3 us (3%)
    dot_general x25, matrix products, contract(): lax.dot_general(left, right, (((left_dim,), (right_dim,)), ((), ())), pre...  87.4 us
    all_to_all x11, waiting for transfers between devices, spread(): lax.all_to_all(jnp.broadcast_to(value[None], (count,) + value.shape), axi...  64.5 us
    all_to_all x11, starting transfers between devices, spread(): lax.all_to_all(jnp.broadcast_to(value[None], (count,) + value.shape), axi...  48.2 us
    reduce_scatter x1, waiting for transfers between devices, local(): lax.psum_scatter(contract(slot_hot_rel, expand_grad, 1, 0).astype(LOW), '...  38.6 us
    all_gather x1, waiting for transfers between devices, local(): lax.all_gather(jnp.concatenate([hidden_weight.astype(LOW), project_weight...  35.4 us
    ppermute x27, waiting for transfers between devices, swap(): lax.ppermute(value, axis, [(at, at ^ bit) for at in range(lax.axis_size(a...  26.3 us
    ppermute x27, starting transfers between devices, swap(): lax.ppermute(value, axis, [(at, at ^ bit) for at in range(lax.axis_size(a...  20.4 us
    all_to_all x1, waiting for transfers between devices, local(): lax.all_to_all(contract(slot_hot, squeeze_grad, 1, 0).astype(LOW).reshape...  16.5 us
  transfers between devices with their start and end apart: 45, of which 20 were waited for; matrix products, arithmetic and copies ran while one was open for 34% of the time, Pallas kernels for 0%

profile of v1, /device:TPU:0, one launch (start us, length us, event | category | flops | bytes accessed | tf_op | source)
XLA Modules:
  0.0 497.2 jit_solution(4380436125449219792)
XLA Ops:
  11.2 7.3 %all-to-all-start = ((bf16[8,512,128]{2,1,0:T(8,128)(2,1)}), bf16[8,512,128]{2,1,0:T(8,128)(2,1)}, u32[]{:S(2)}, u32[]{:S(2)}) async-start(bf16[8,512,128]{2,1,0:T(8,128)(2,1)} %broadcast_in_dim.28), calls=%async_computation | async-start | bytes 2097152 | tf_op jit(solution)/shard_map/all_to_all | solution.py:33
  19.3 31.7 %all-to-all-done = bf16[8,512,128]{2,1,0:T(8,128)(2,1)} async-done(((bf16[8,512,128]{2,1,0:T(8,128)(2,1)}), bf16[8,512,128]{2,1,0:T(8,128)(2,1)}, u32[]{:S(2)}, u32[]{:S(2)}) %all-to-all-start) | async-done | bytes 1048608 | tf_op jit(solution)/shard_map/all_to_all | solution.py:33
  51.0 8.7 %fusion.24 = bf16[2048,128]{0,1:T(8,128)(2,1)S(1)} fusion(bf16[4096,128]{1,0:T(8,128)(2,1)} %bitcast, s32[4096]{0:T(1024)S(1)} %copy-done.62), kind=kOutput, calls=%fused_computation.53 | convolution fusion | flops 2156134400 | bytes 1589248 | tf_op jit(solution)/shard_map/dot_general | solution.py:21
  82.0 3.9 fusion.148
  87.7 5.7 %all-to-all-start.2 = ((f32[8,2,128]{2,1,0:T(2,128)}), f32[8,2,128]{2,1,0:T(2,128)S(1)}, u32[]{:S(2)}, u32[]{:S(2)}) async-start(f32[8,2,128]{2,1,0:T(2,128)} %broadcast_in_dim.30), calls=%async_computation.2 | async-start | bytes 16384 | tf_op jit(solution)/shard_map/all_to_all | solution.py:33
  95.0 10.9 %iota_compare_fusion.2 = pred[2048,4096]{1,0:T(32,128)(4,1)} fusion(s32[4096]{0:T(1024)S(1)} %copy-done.62), kind=kLoop, calls=%fused_computation.2 | loop fusion | flops 8388608 | bytes 8404992 | tf_op jit(solution)/shard_map/eq | solution.py:145
  107.8 8.9 %fusion.25 = bf16[2048,128]{0,1:T(8,128)(2,1)S(1)} fusion(bf16[4096,128]{1,0:T(8,128)(2,1)} %all-gather.7.cloned.1.call-done, s32[4096]{0:T(1024)S(1)} %copy-done.62), kind=kOutput, calls=%fused_computation.54 | convolution fusion | flops 2156134400 | bytes 1589248 | tf_op jit(solution)/shard_map/dot_general | solution.py:21
  129.4 6.0 %all-to-all-start.3 = ((f32[8,2,512]{2,1,0:T(2,128)}), f32[8,2,512]{2,1,0:T(2,128)S(1)}, u32[]{:S(2)}, u32[]{:S(2)}) async-start(f32[8,2,512]{2,1,0:T(2,128)} %broadcast_in_dim.31), calls=%async_computation.3 | async-start | bytes 65536 | tf_op jit(solution)/shard_map/all_to_all | solution.py:33
  135.4 6.7 %all-to-all-done.3 = f32[8,2,512]{2,1,0:T(2,128)S(1)} async-done(((f32[8,2,512]{2,1,0:T(2,128)}), f32[8,2,512]{2,1,0:T(2,128)S(1)}, u32[]{:S(2)}, u32[]{:S(2)}) %all-to-all-start.3) | async-done | bytes 32800 | tf_op jit(solution)/shard_map/all_to_all | solution.py:33
  142.7 5.0 %fusion.140 = (bf16[1568,512]{1,0:T(8,128)(2,1)}, f32[1568,512]{1,0:T(8,128)}) fusion(bf16[1568,2048]{1,0:T(8,128)(2,1)} %bitcast.274, s32[]{:T(128)S(6)} %select_n.86, f32[512]{0:T(512)S(1)} %bitcast.318, f32[512]{0:T(512)S(1)} %bitcast.320, f32[512]{0:T(512)S(1)} %bitcast.312, f32[1568,512]{1,0:T(8,128)S(1)} %get-tuple-element.205, f32[512]{0:T(512)S(1)} %bitcast.315), kind=kLoop, calls=%fused_computation.316 | loop fusion | flops 8830976 | bytes 9641988 | tf_op jit(solution)/shard_map/convert_element_type | solution.py:221
  149.9 5.4 %all_gather.20 = bf16[32,2048]{1,0:T(8,128)(2,1)S(1)} all-gather(bf16[32,512]{1,0:T(8,128)(2,1)S(1)} %multiply_convert_fusion.11), channel_id=1, replica_groups=mesh['dp'=8,'chan'=4] {'chan'}, dimensions={1}, use_global_device_ids=true | all-gather | bytes 163840 | tf_op jit(solution)/shard_map/all_gather | solution.py:224
  155.3 35.4 %all-gather.9.cloned.1.call-done = bf16[4096,640]{1,0:T(8,128)(2,1)} async-done(((bf16[512,640]{1,0:T(8,128)(2,1)}), bf16[4096,640]{1,0:T(8,128)(2,1)}) %all-gather.9.cloned.1.call-update) | async-done | bytes 5242896 | tf_op jit(solution)/shard_map/all_gather | solution.py:156
  190.7 11.2 %fusion.21 = bf16[2048,512]{1,0:T(8,128)(2,1)S(1)} fusion(bf16[4096,640]{1,0:T(8,128)(2,1)} %all-gather.9.cloned.1.call-done, s32[4096]{0:T(1024)S(1)} %copy-done.62), kind=kOutput, calls=%fused_computation.49 | convolution fusion | flops 8599371776 | bytes 6307840 | tf_op jit(solution)/shard_map/dot_general | solution.py:21
  217.2 4.6 all-to-all-start.4
  224.6 4.4 all-to-all-done.4
  236.5 5.0 %fusion.135 = (f32[480]{0:T(512)S(1)}, f32[480,3000]{1,0:T(8,128)S(1)}) fusion(f32[3000]{0:T(1024)S(1)} %add.443, f32[480]{0:T(512)S(1)} %get-tuple-element.124, f32[480,3000]{1,0:T(8,128)} %get-tuple-element.208), kind=kLoop, calls=%fused_computation.313 | loop fusion | flops 5759520 | bytes 11535840 | tf_op jit(solution)/shard_map/reduce_sum | solution.py:264
  259.9 3.8 multiply_reduce_fusion
  264.4 4.1 all-to-all-start.7
  269.6 6.1 %all-to-all-done.7 = f32[8,1,3000]{2,1,0:T(1,128)S(1)} async-done(((f32[8,1,3000]{2,1,0:T(1,128)}), f32[8,1,3000]{2,1,0:T(1,128)S(1)}, u32[]{:S(2)}, u32[]{:S(2)}) %all-to-all-start.7) | async-done | bytes 96032 | tf_op jit(solution)/shard_map/all_to_all | solution.py:33
  289.0 6.0 %multiply_subtract_fusion.1 = (f32[512,512]{1,0:T(8,128)}, f32[512,512]{1,0:T(8,128)}, f32[512,512]{1,0:T(8,128)}) fusion(f32[512,512]{1,0:T(8,128)} %param.40, f32[]{:T(128)} %bitcast.102, f32[512,512]{1,0:T(8,128)} %param.42, f32[512,512]{1,0:T(8,128)} %param.41, bf16[256,512]{1,0:T(8,128)(2,1)} %copy-done.49, ...), kind=kOutput, calls=%fused_computation.91 | convolution fusion | flops 675938304 | bytes 7604228 | tf_op jit(solution)/shard_map/dot_general | solution.py:21
  296.0 4.2 fusion.117
  306.1 4.7 all-to-all-done.8
  315.3 7.9 %all_gather.23 = bf16[2048,128]{1,0:T(8,128)(2,1)} all-gather(bf16[512,128]{1,0:T(8,128)(2,1)S(1)} %convolution_convert_fusion.3), channel_id=1, replica_groups=mesh['dp'=8,'chan'=4] {'chan'}, dimensions={0}, use_global_device_ids=true | all-gather | bytes 655360 | tf_op jit(solution)/shard_map/all_gather | solution.py:305
  329.8 8.6 %collective-permute-done.16 = bf16[1,1568,128]{2,1,0:T(8,128)(2,1)S(1)} collective-permute-done((bf16[1,1568,128]{2,1,0:T(8,128)(2,1)S(1)}, bf16[1,1568,128]{2,1,0:T(8,128)(2,1)S(1)}, u32[]{:S(2)}, u32[]{:S(2)}) %collective-permute-start.16) | collective-permute-done | bytes 401440 | tf_op jit(solution)/shard_map/ppermute | solution.py:41
  356.9 8.0 %fusion.14 = bf16[4096,128]{1,0:T(8,128)(2,1)} fusion(s32[4096]{0:T(1024)S(1)} %broadcast_xor_fusion, bf16[512,128]{1,0:T(8,128)(2,1)} %collective-permute-done.26, bf16[512,128]{1,0:T(8,128)(2,1)} %collective-permute-done.25, bf16[512,128]{1,0:T(8,128)(2,1)} %collective-permute-done.24, bf16[512,128]{1,0:T(8,128)(2,1)S(1)} %get-tuple-element.157), kind=kOutput, calls=%fused_computation.21 | convolution fusion | flops 2158493696 | bytes 1589248 | tf_op jit(solution)/shard_map/dot_general | solution.py:21
  369.9 4.5 convolution_convert_fusion.1
  375.7 4.9 collective-permute-done.18
  387.0 38.6 %reduce-scatter.2.cloned.1.call-done = bf16[512,128]{1,0:T(8,128)(2,1)} async-done(((bf16[4096,128]{1,0:T(8,128)(2,1)}), bf16[512,128]{1,0:T(8,128)(2,1)}) %reduce-scatter.2.cloned.1.call-update) | async-done | bytes 131088 | tf_op jit(solution)/shard_map/reduce_scatter | solution.py:344
  433.5 4.0 convolution_convert_fusion.clone.5
  437.5 7.2 %fusion.15 = bf16[4096,128]{1,0:T(8,128)(2,1)} fusion(s32[4096]{0:T(1024)S(1)} %copy-done.62, bf16[128,2048]{1,0:T(8,128)(2,1)S(1)} %convolution_convert_fusion.clone.5), kind=kOutput, calls=%fused_computation.22 | convolution fusion | flops 2156396544 | bytes 1589248 | tf_op jit(solution)/shard_map/dot_general | solution.py:21
  445.7 13.1 %all-to-all-done.12 = bf16[8,576,128]{2,1,0:T(8,128)(2,1)S(1)} async-done(((bf16[8,576,128]{2,1,0:T(8,128)(2,1)}), bf16[8,576,128]{2,1,0:T(8,128)(2,1)S(1)}, u32[]{:S(2)}, u32[]{:S(2)}) %all-to-all-start.12) | async-done | bytes 1179680 | tf_op jit(solution)/shard_map/all_to_all | solution.py:367
  471.6 16.5 %all-to-all-done.11 = bf16[8,512,128]{2,1,0:T(8,128)(2,1)S(1)} async-done(((bf16[8,512,128]{2,1,0:T(8,128)(2,1)}), bf16[8,512,128]{2,1,0:T(8,128)(2,1)S(1)}, u32[]{:S(2)}, u32[]{:S(2)}) %all-to-all-start.11) | async-done | bytes 1048608 | tf_op jit(solution)/shard_map/all_to_all | solution.py:380
  (438 shorter events, 175.2 us)
Async XLA Ops:
  7.2 72.2 %all-gather.5.cloned.1.call-start = ((), (), s32[]{:S(2)}) async-start(), calls=%async_computation.14 | async-start | bytes 1327104 | tf_op jit(solution)/shard_map/all_gather | solution.py:154
  11.2 39.8 %all-to-all-start = ((bf16[8,512,128]{2,1,0:T(8,128)(2,1)}), bf16[8,512,128]{2,1,0:T(8,128)(2,1)}, u32[]{:S(2)}, u32[]{:S(2)}) async-start(bf16[8,512,128]{2,1,0:T(8,128)(2,1)} %broadcast_in_dim.28), calls=%async_computation | async-start | bytes 2097152 | tf_op jit(solution)/shard_map/all_to_all | solution.py:33
  18.4 89.4 %all-gather.7.cloned.1.call-start = ((), (), s32[]{:S(2)}) async-start(), calls=%async_computation.15 | async-start | bytes 1179648 | tf_op jit(solution)/shard_map/all_gather | solution.py:155
  63.1 10.0 %all-to-all-start.1 = ((f32[8,2,128]{2,1,0:T(2,128)}), f32[8,2,128]{2,1,0:T(2,128)S(1)}, u32[]{:S(2)}, u32[]{:S(2)}) async-start(f32[8,2,128]{2,1,0:T(2,128)} %broadcast_in_dim.29), calls=%async_computation.1 | async-start | bytes 16384 | tf_op jit(solution)/shard_map/all_to_all | solution.py:33
  66.6 124.2 %all-gather.9.cloned.1.call-start = ((), (), s32[]{:S(2)}) async-start(), calls=%async_computation.16 | async-start | bytes 5898240 | tf_op jit(solution)/shard_map/all_gather | solution.py:156
  67.7 10.6 %collective-permute-start = (bf16[1,1568,128]{2,1,0:T(8,128)(2,1)S(1)}, bf16[1,1568,128]{2,1,0:T(8,128)(2,1)S(1)}, u32[]{:S(2)}, u32[]{:S(2)}) collective-permute-start(bf16[1,1568,128]{2,1,0:T(8,128)(2,1)S(1)} %bitcast.290), channel_id=1, source_target_pairs={{0,2},{1,3},{2,0},{3,1},{4,6},{5,7},{6,4},{7,5},{8,10},{9,11},{10,... | collective-permute-start | bytes 1204232 | tf_op jit(solution)/shard_map/ppermute | solution.py:41
  87.7 18.9 %all-to-all-start.2 = ((f32[8,2,128]{2,1,0:T(2,128)}), f32[8,2,128]{2,1,0:T(2,128)S(1)}, u32[]{:S(2)}, u32[]{:S(2)}) async-start(f32[8,2,128]{2,1,0:T(2,128)} %broadcast_in_dim.30), calls=%async_computation.2 | async-start | bytes 16384 | tf_op jit(solution)/shard_map/all_to_all | solution.py:33
  93.3 14.3 %collective-permute-start.4 = (bf16[1,1568,128]{2,1,0:T(8,128)(2,1)S(1)}, bf16[1,1568,128]{2,1,0:T(8,128)(2,1)S(1)}, u32[]{:S(2)}, u32[]{:S(2)}) collective-permute-start(bf16[1,1568,128]{2,1,0:T(8,128)(2,1)S(1)} %bitcast.296), channel_id=1, source_target_pairs={{0,2},{1,3},{2,0},{3,1},{4,6},{5,7},{6,4},{7,5},{8,10},{9,11},{10,... | collective-permute-start | bytes 1204232 | tf_op jit(solution)/shard_map/ppermute | solution.py:41
  107.7 11.9 %collective-permute-start.5 = (bf16[2,1568,128]{2,1,0:T(8,128)(2,1)S(1)}, bf16[2,1568,128]{2,1,0:T(8,128)(2,1)S(1)}, u32[]{:S(2)}, u32[]{:S(2)}) collective-permute-start(bf16[2,1568,128]{2,1,0:T(8,128)(2,1)S(1)} %pad_maximum_fusion.3), channel_id=1, source_target_pairs={{0,1},{1,0},{2,3},{3,2},{4,5},{5,4},{6,7},{7,6},{8,9},{9,8},{10,11... | collective-permute-start | bytes 2408456 | tf_op jit(solution)/shard_map/ppermute | solution.py:41
  129.4 12.7 %all-to-all-start.3 = ((f32[8,2,512]{2,1,0:T(2,128)}), f32[8,2,512]{2,1,0:T(2,128)S(1)}, u32[]{:S(2)}, u32[]{:S(2)}) async-start(f32[8,2,512]{2,1,0:T(2,128)} %broadcast_in_dim.31), calls=%async_computation.3 | async-start | bytes 65536 | tf_op jit(solution)/shard_map/all_to_all | solution.py:33
  204.5 12.0 %all-to-all-start.5 = ((bf16[8,32,512]{2,1,0:T(8,128)(2,1)}), bf16[8,32,512]{2,1,0:T(8,128)(2,1)S(1)}, u32[]{:S(2)}, u32[]{:S(2)}) async-start(bf16[8,32,512]{2,1,0:T(8,128)(2,1)} %broadcast_in_dim.33), calls=%async_computation.5 | async-start | bytes 524288 | tf_op jit(solution)/shard_map/all_to_all | solution.py:33
  217.2 11.7 %all-to-all-start.4 = ((f32[8,1,3032]{2,1,0:T(1,128)}), f32[8,1,3032]{2,1,0:T(1,128)S(1)}, u32[]{:S(2)}, u32[]{:S(2)}) async-start(f32[8,1,3032]{2,1,0:T(1,128)} %broadcast_in_dim.32), calls=%async_computation.4 | async-start | bytes 196608 | tf_op jit(solution)/shard_map/all_to_all | solution.py:33
  221.8 67.1 %all-gather.11.cloned.1.call-start = ((), (), s32[]{:S(2)}) async-start(), calls=%async_computation.18 | async-start | bytes 1179648 | tf_op jit(solution)/shard_map/all_gather | solution.py:225
  245.6 10.8 %all-to-all-start.6 = ((f32[8,1,3000]{2,1,0:T(1,128)}), f32[8,1,3000]{2,1,0:T(1,128)S(1)}, u32[]{:S(2)}, u32[]{:S(2)}) async-start(f32[8,1,3000]{2,1,0:T(1,128)} %broadcast_in_dim.34), calls=%async_computation.6 | async-start | bytes 196608 | tf_op jit(solution)/shard_map/all_to_all | solution.py:33
  264.4 11.2 %all-to-all-start.7 = ((f32[8,1,3000]{2,1,0:T(1,128)}), f32[8,1,3000]{2,1,0:T(1,128)S(1)}, u32[]{:S(2)}, u32[]{:S(2)}) async-start(f32[8,1,3000]{2,1,0:T(1,128)} %broadcast_in_dim.35), calls=%async_computation.7 | async-start | bytes 196608 | tf_op jit(solution)/shard_map/all_to_all | solution.py:33
  286.4 181.4 %collective-permute-start.21 = (bf16[512,128]{0,1:T(8,128)(2,1)}, bf16[512,128]{0,1:T(8,128)(2,1)}, u32[]{:S(2)}, u32[]{:S(2)}) collective-permute-start(bf16[512,128]{0,1:T(8,128)(2,1)} %get-tuple-element.164), channel_id=1, source_target_pairs={{0,1},{1,0},{2,3},{3,2},{4,5},{5,4},{6,7},{7,6},{8,9},{9,8},{10,11... | collective-permute-start | bytes 393224 | tf_op jit(solution)/shard_map/ppermute | solution.py:41
  286.9 180.9 %collective-permute-start.22 = (bf16[512,128]{0,1:T(8,128)(2,1)}, bf16[512,128]{0,1:T(8,128)(2,1)}, u32[]{:S(2)}, u32[]{:S(2)}) collective-permute-start(bf16[512,128]{0,1:T(8,128)(2,1)} %get-tuple-element.163), channel_id=1, source_target_pairs={{0,2},{1,3},{2,0},{3,1},{4,6},{5,7},{6,4},{7,5},{8,10},{9,11},{10,... | collective-permute-start | bytes 393224 | tf_op jit(solution)/shard_map/ppermute | solution.py:41
  300.9 10.0 %all-to-all-start.8 = ((f32[8,2,512]{2,1,0:T(2,128)}), f32[8,2,512]{2,1,0:T(2,128)S(1)}, u32[]{:S(2)}, u32[]{:S(2)}) async-start(f32[8,2,512]{2,1,0:T(2,128)} %broadcast_in_dim.38), calls=%async_computation.8 | async-start | bytes 65536 | tf_op jit(solution)/shard_map/all_to_all | solution.py:33
  315.2 11.5 %collective-permute-start.15 = (bf16[2,1568,128]{2,1,0:T(8,128)(2,1)S(1)}, bf16[2,1568,128]{2,1,0:T(8,128)(2,1)S(1)}, u32[]{:S(2)}, u32[]{:S(2)}) collective-permute-start(bf16[2,1568,128]{2,1,0:T(8,128)(2,1)S(1)} %pad_maximum_fusion.4), channel_id=1, source_target_pairs={{0,1},{1,0},{2,3},{3,2},{4,5},{5,4},{6,7},{7,6},{8,9},{9,8},{10,11... | collective-permute-start | bytes 2408456 | tf_op jit(solution)/shard_map/ppermute | solution.py:41
  326.9 11.6 %collective-permute-start.16 = (bf16[1,1568,128]{2,1,0:T(8,128)(2,1)S(1)}, bf16[1,1568,128]{2,1,0:T(8,128)(2,1)S(1)}, u32[]{:S(2)}, u32[]{:S(2)}) collective-permute-start(bf16[1,1568,128]{2,1,0:T(8,128)(2,1)S(1)} %fusion.78), channel_id=1, source_target_pairs={{0,2},{1,3},{2,0},{3,1},{4,6},{5,7},{6,4},{7,5},{8,10},{9,11},{10,... | collective-permute-start | bytes 1204232 | tf_op jit(solution)/shard_map/ppermute | solution.py:41
  343.0 82.6 %reduce-scatter.2.cloned.1.call-start = ((), (), s32[]{:S(2)}) async-start(), calls=%async_computation.17 | async-start | bytes 1179648 | tf_op jit(solution)/shard_map/reduce_scatter | solution.py:344
  344.0 11.3 %collective-permute-start.24 = (bf16[512,128]{1,0:T(8,128)(2,1)}, bf16[512,128]{1,0:T(8,128)(2,1)}, u32[]{:S(2)}, u32[]{:S(2)}) collective-permute-start(bf16[512,128]{1,0:T(8,128)(2,1)} %get-tuple-element.160), channel_id=1, source_target_pairs={{0,1},{1,0},{2,3},{3,2},{4,5},{5,4},{6,7},{7,6},{8,9},{9,8},{10,11... | collective-permute-start | bytes 393224 | tf_op jit(solution)/shard_map/ppermute | solution.py:41
  344.0 11.3 %collective-permute-start.25 = (bf16[512,128]{1,0:T(8,128)(2,1)}, bf16[512,128]{1,0:T(8,128)(2,1)}, u32[]{:S(2)}, u32[]{:S(2)}) collective-permute-start(bf16[512,128]{1,0:T(8,128)(2,1)} %get-tuple-element.159), channel_id=1, source_target_pairs={{0,2},{1,3},{2,0},{3,1},{4,6},{5,7},{6,4},{7,5},{8,10},{9,11},{10,... | collective-permute-start | bytes 393224 | tf_op jit(solution)/shard_map/ppermute | solution.py:41
  345.5 11.4 %collective-permute-start.26 = (bf16[512,128]{1,0:T(8,128)(2,1)}, bf16[512,128]{1,0:T(8,128)(2,1)}, u32[]{:S(2)}, u32[]{:S(2)}) collective-permute-start(bf16[512,128]{1,0:T(8,128)(2,1)} %get-tuple-element.158), channel_id=1, source_target_pairs={{0,3},{1,2},{2,1},{3,0},{4,7},{5,6},{6,5},{7,4},{8,11},{9,10},{10,... | collective-permute-start | bytes 393224 | tf_op jit(solution)/shard_map/ppermute | solution.py:41
  355.3 112.4 %collective-permute-start.23 = (bf16[512,128]{0,1:T(8,128)(2,1)}, bf16[512,128]{0,1:T(8,128)(2,1)}, u32[]{:S(2)}, u32[]{:S(2)}) collective-permute-start(bf16[512,128]{0,1:T(8,128)(2,1)} %get-tuple-element.162), channel_id=1, source_target_pairs={{0,3},{1,2},{2,1},{3,0},{4,7},{5,6},{6,5},{7,4},{8,11},{9,10},{10,... | collective-permute-start | bytes 393224 | tf_op jit(solution)/shard_map/ppermute | solution.py:41
  355.3 12.8 %collective-permute-start.17 = (bf16[2,1568,128]{2,1,0:T(8,128)(2,1)}, bf16[2,1568,128]{2,1,0:T(8,128)(2,1)}, u32[]{:S(2)}, u32[]{:S(2)}) collective-permute-start(bf16[2,1568,128]{2,1,0:T(8,128)(2,1)} %pad_maximum_fusion.5), channel_id=1, source_target_pairs={{0,1},{1,0},{2,3},{3,2},{4,5},{5,4},{6,7},{7,6},{8,9},{9,8},{10,11... | collective-permute-start | bytes 2408456 | tf_op jit(solution)/shard_map/ppermute | solution.py:41
  369.3 11.3 %collective-permute-start.18 = (bf16[1,1568,128]{2,1,0:T(8,128)(2,1)S(1)}, bf16[1,1568,128]{2,1,0:T(8,128)(2,1)S(1)}, u32[]{:S(2)}, u32[]{:S(2)}) collective-permute-start(bf16[1,1568,128]{2,1,0:T(8,128)(2,1)S(1)} %fusion.79), channel_id=1, source_target_pairs={{0,2},{1,3},{2,0},{3,1},{4,6},{5,7},{6,4},{7,5},{8,10},{9,11},{10,... | collective-permute-start | bytes 1204232 | tf_op jit(solution)/shard_map/ppermute | solution.py:41
  383.6 44.1 %all-to-all-start.10 = ((f32[8,2,128]{2,1,0:T(2,128)}), f32[8,2,128]{2,1,0:T(2,128)S(1)}, u32[]{:S(2)}, u32[]{:S(2)}) async-start(f32[8,2,128]{2,1,0:T(2,128)} %broadcast_in_dim.40), calls=%async_computation.10 | async-start | bytes 16384 | tf_op jit(solution)/shard_map/all_to_all | solution.py:33
  427.8 31.0 %all-to-all-start.12 = ((bf16[8,576,128]{2,1,0:T(8,128)(2,1)}), bf16[8,576,128]{2,1,0:T(8,128)(2,1)S(1)}, u32[]{:S(2)}, u32[]{:S(2)}) async-start(bf16[8,576,128]{2,1,0:T(8,128)(2,1)} %bitcast.289), calls=%async_computation.12 | async-start | bytes 2359296 | tf_op jit(solution)/shard_map/all_to_all | solution.py:367
  432.0 12.7 %collective-permute-start.19 = (bf16[1,1568,128]{2,1,0:T(8,128)(2,1)S(1)}, bf16[1,1568,128]{2,1,0:T(8,128)(2,1)S(1)}, u32[]{:S(2)}, u32[]{:S(2)}) collective-permute-start(bf16[1,1568,128]{2,1,0:T(8,128)(2,1)S(1)} %bitcast.287), channel_id=1, source_target_pairs={{0,2},{1,3},{2,0},{3,1},{4,6},{5,7},{6,4},{7,5},{8,10},{9,11},{10,... | collective-permute-start | bytes 1204232 | tf_op jit(solution)/shard_map/ppermute | solution.py:41
  445.7 20.8 %collective-permute-start.20 = (bf16[2,1568,128]{2,1,0:T(8,128)(2,1)}, bf16[2,1568,128]{2,1,0:T(8,128)(2,1)}, u32[]{:S(2)}, u32[]{:S(2)}) collective-permute-start(bf16[2,1568,128]{2,1,0:T(8,128)(2,1)} %pad_maximum_fusion.6), channel_id=1, source_target_pairs={{0,1},{1,0},{2,3},{3,2},{4,5},{5,4},{6,7},{7,6},{8,9},{9,8},{10,11... | collective-permute-start | bytes 2408456 | tf_op jit(solution)/shard_map/ppermute | solution.py:41
  458.8 29.4 %all-to-all-start.11 = ((bf16[8,512,128]{2,1,0:T(8,128)(2,1)}), bf16[8,512,128]{2,1,0:T(8,128)(2,1)S(1)}, u32[]{:S(2)}, u32[]{:S(2)}) async-start(bf16[8,512,128]{2,1,0:T(8,128)(2,1)} %bitcast.301), calls=%async_computation.11 | async-start | bytes 2097152 | tf_op jit(solution)/shard_map/all_to_all | solution.py:380
  (118 other events, 1286.1 us)
Sparse Core Ops, SparseCore 0:
  10.8 50.4 all-gather.4
  64.0 38.8 all-gather.6
  105.7 85.0 all-gather.8
  231.1 37.4 all-gather.10
  365.0 60.5 reduce-scatter.1
